TPU v7x, 32 devices: a whole 2x2x4 slice. The times are simulated.
32 devices in a mesh: dp: 4 (over z), shard: 8 (over y, x, core).
Axes of the slice: x: 2, y: 2, z: 4, core: 2. Of those that a mesh axis runs over, the one named last changes fastest.
Arguments:
- hidden_in: bfloat16 [4096, 5120], P('dp', 'shard'), may hold values from -6 to 6
- context_in: bfloat16 [4096, 5120], P('dp', 'shard'), may hold values from -6 to 6
- query_cotan: bfloat16 [4096, 2560], P('dp', 'shard'), may hold values from -0.1875 to 0.1875
- output_cotan: bfloat16 [4096, 2560], P('dp', 'shard'), may hold values from -0.1875 to 0.1875
- query_error: bfloat16 [4, 5120, 2560], P('dp', 'shard'), may hold values from -3 to 3
- output_error: bfloat16 [4, 5120, 2560], P('dp', 'shard'), may hold values from -3 to 3
- query_weight: float32 [5120, 2560], P('shard', 'dp'), may hold values from -0.6 to 0.6
- output_weight: float32 [5120, 2560], P('shard', 'dp'), may hold values from -0.6 to 0.6
- start_factors: bfloat16 [2, 2560, 32], replicated, may hold values from -0.09863281 to 0.09863281
Outputs:
- query_error_new: bfloat16 [4, 5120, 2560], P('dp', 'shard')
- output_error_new: bfloat16 [4, 5120, 2560], P('dp', 'shard')
- query_weight_new: float32 [5120, 2560], P('shard', 'dp')
- output_weight_new: float32 [5120, 2560], P('shard', 'dp')
All inputs are finite; a program needn't handle non-finite values.
Results may differ from a plain program's by a relative error of at most 0.005.
Values may be sent and summed in bfloat16 or wider, within the bound.
A program may use at most 128 MiB of HBM per device.

v0:
```python
import functools

import jax
import jax.numpy as jnp
from jax import lax
from jax.experimental import pallas as pl
from jax.experimental.pallas import tpu as pltpu
from jax.sharding import PartitionSpec as P

HIGH = lax.Precision.HIGHEST


def contract_tokens(left_op, right_op):
    return lax.dot_general(
        left_op, right_op, (((0,), (0,)), ((), ())), preferred_element_type=jnp.float32
    )


def form_grads(hidden_in, context_in, query_cotan, output_cotan):

    def query_part(piece, start):
        return contract_tokens(hidden_in, piece)

    def output_part(piece, start):
        return contract_tokens(context_in, piece)

    query_grad = query_part(lax.all_gather(query_cotan, "shard", axis=1, tiled=True), jnp.int32(0))
    output_grad = output_part(
        lax.all_gather(output_cotan, "shard", axis=1, tiled=True), jnp.int32(0)
    )
    return (query_grad, output_grad)


def orthonormal(left, gram):
    chol = jnp.linalg.cholesky(gram)
    return lax.linalg.triangular_solve(chol, left, left_side=False, lower=True, transpose_a=True)


def body(
    hidden_in,
    context_in,
    query_cotan,
    output_cotan,
    query_error,
    output_error,
    query_weight,
    output_weight,
    start_factors,
):
    replicas = lax.axis_size("dp")
    query_start = start_factors[0].astype(jnp.float32)
    output_start = start_factors[1].astype(jnp.float32)
    query_prior = query_error[0].astype(jnp.float32)
    output_prior = output_error[0].astype(jnp.float32)
    query_grad, output_grad = form_grads(hidden_in, context_in, query_cotan, output_cotan)
    query_full = query_grad + query_prior
    output_full = output_grad + output_prior
    query_left = jnp.dot(query_full, query_start, precision=HIGH)
    output_left = jnp.dot(output_full, output_start, precision=HIGH)
    query_left, output_left = lax.psum((query_left, output_left), "dp")
    query_left = query_left / jnp.float32(replicas)
    output_left = output_left / jnp.float32(replicas)
    query_gram, output_gram = lax.psum(
        (
            jnp.dot(query_left.T, query_left, precision=HIGH),
            jnp.dot(output_left.T, output_left, precision=HIGH),
        ),
        "shard",
    )
    query_ortho = orthonormal(query_left, query_gram)
    output_ortho = orthonormal(output_left, output_gram)
    query_term = jnp.dot(query_full.T, query_ortho, precision=HIGH)
    output_term = jnp.dot(output_full.T, output_ortho, precision=HIGH)
    query_part, output_part = (
        lax.psum_scatter(
            query_term.astype(jnp.bfloat16), "shard", scatter_dimension=0, tiled=True
        ).astype(jnp.float32),
        lax.psum_scatter(
            output_term.astype(jnp.bfloat16), "shard", scatter_dimension=0, tiled=True
        ).astype(jnp.float32),
    )
    query_part, output_part = lax.psum((query_part, output_part), "dp")
    query_right, output_right = (
        lax.all_gather(query_part, "shard", axis=0, tiled=True),
        lax.all_gather(output_part, "shard", axis=0, tiled=True),
    )
    query_right = query_right / jnp.float32(replicas)
    output_right = output_right / jnp.float32(replicas)
    query_approx = jnp.dot(query_ortho, query_right.T, precision=HIGH)
    output_approx = jnp.dot(output_ortho, output_right.T, precision=HIGH)
    query_error_new = (query_full - query_approx).astype(jnp.bfloat16)[None]
    output_error_new = (output_full - output_approx).astype(jnp.bfloat16)[None]
    weight_cols = query_weight.shape[1]
    col_start = lax.axis_index("dp") * weight_cols
    query_cols = lax.dynamic_slice_in_dim(query_approx, col_start, weight_cols, 1)
    output_cols = lax.dynamic_slice_in_dim(output_approx, col_start, weight_cols, 1)
    return (
        query_error_new,
        output_error_new,
        query_weight - query_cols,
        output_weight - output_cols,
    )


NT = (((1,), (1,)), ((), ()))
NN = (((1,), (0,)), ((), ()))
TN = (((0,), (0,)), ((), ()))
MESH = pl.DeviceIdType.MESH


def mxu(lhs, rhs, dims):
    return lax.dot_general(lhs, rhs, dims, preferred_element_type=jnp.float32)


def two_terms(value):
    high = value.astype(jnp.bfloat16)
    low = (value - high.astype(jnp.float32)).astype(jnp.bfloat16)
    return jnp.concatenate([high, low], axis=0)


def split_dot(value, rhs, dims):
    rows = value.shape[0]
    both = mxu(two_terms(value), rhs, dims)
    return both[:rows] + both[rows:]


def spd_inverse(gram):
    size = gram.shape[0]
    row_id = lax.broadcasted_iota(jnp.int32, (size, size), 0)
    col_id = lax.broadcasted_iota(jnp.int32, (size, size), 1)
    value = gram
    for k in range(size):
        row = value[k : k + 1, :]
        col = value[:, k : k + 1]
        inv = 1.0 / value[k : k + 1, k : k + 1]
        scaled = row * inv
        rest = value - col * scaled
        rest = jnp.where(col_id == k, -col * inv, rest)
        value = jnp.where(row_id == k, jnp.where(col_id == k, inv, scaled), rest)
    return value


def chain_kernel(
    n, reps,
    a0_hbm, a1_hbm, b0, b1, e0_hbm, e1_hbm, st, sloc,
    g0, g1, at0, at1, lg, rf,
    a0, a1, e0, e1, ps, pr, pf, ls, lr, lf, qs, qr, qf, ts, tr, gs, gr, rs, rr, rd,
    load_sem, own_send, own_recv, fwd_send, fwd_recv, core_send, core_recv,
    ps_s, ps_r, pg_s, pg_r, ls_s, ls_r, lg_s, lg_r,
    qs_s, qs_r, qg_s, qg_r, ts_s, ts_r, gs_s, gs_r,
    rs_s, rs_r, rg_s, rg_r, rf_s, rf_r,
):
    me = lax.axis_index("shard")
    z = lax.axis_index("dp")
    rank = st.shape[1]
    rows = 2 * rank // reps
    acts, errs, cots, gathered = (a0, a1), (e0, e1), (b0, b1), (g0, g1)
    half = b0.shape[0] // 2

    loads = [
        pltpu.make_async_copy(src, dst, load_sem.at[i])
        for i, (src, dst) in enumerate(
            ((e0_hbm, e0), (e1_hbm, e1), (a0_hbm, a0), (a1_hbm, a1), (b0, g0.at[me]), (b1, g1.at[me]))
        )
    ]
    for load in loads:
        load.start()

    barrier = pltpu.get_barrier_semaphore()
    for k in range(1, n):
        pl.semaphore_signal(barrier, inc=1, device_id=(z, lax.rem(me + k, n)), device_id_type=MESH)
    for k in range(1, reps):
        pl.semaphore_signal(barrier, inc=1, device_id=(lax.rem(z + k, reps), me), device_id_type=MESH)
    pl.semaphore_wait(barrier, n - 1 + reps - 1)

    def remote(src, dst, ss, rsem, target):
        return pltpu.make_async_remote_copy(
            src_ref=src, dst_ref=dst, send_sem=ss, recv_sem=rsem,
            device_id=target, device_id_type=MESH,
        )

    def shard_peer(k):
        return (z, lax.rem(me + k, n))

    def dp_peer(k):
        return (lax.rem(z + k, reps), me)

    def start(copies):
        for copy in copies:
            copy.start()
        return copies

    def arrived(copies):
        for copy in copies:
            copy.wait_recv()

    def scatter(src, dst, ss, rsem):
        return start([
            remote(src.at[lax.rem(me + k, n)], dst.at[k - 1], ss.at[k - 1], rsem.at[k - 1], shard_peer(k))
            for k in range(1, n)
        ])

    def spread(buf, ss, rsem):
        return start([
            remote(buf.at[me], buf.at[me], ss.at[k - 1], rsem.at[k - 1], shard_peer(k))
            for k in range(1, n)
        ])

    def total(own, parts, count):
        value = own
        for k in range(count):
            value = value + parts[k].astype(jnp.float32)
        return value

    def dp_scatter(src, dst, ss, rsem):
        return start([
            remote(
                src.at[pl.ds(pl.multiple_of(lax.rem(z + k, reps) * rows, rows), rows)],
                dst.at[k - 1], ss.at[k - 1], rsem.at[k - 1], dp_peer(k),
            )
            for k in range(1, reps)
        ])

    mine = pl.ds(pl.multiple_of(z * rows, rows), rows)

    def dp_spread(buf, ss, rsem):
        return start([
            remote(buf.at[mine], buf.at[mine], ss.at[k - 1], rsem.at[k - 1], dp_peer(k))
            for k in range(1, reps)
        ])

    c = lax.rem(me, 2)
    x = lax.rem(me // 2, 2)
    y = me // 4
    at_c = me + 1 - 2 * c
    at_x = me + 2 - 4 * x
    at_y = me + 4 - 8 * y
    at_d = at_x + 4 - 8 * y
    pending = []

    token_piece = ps.shape[2]
    for p in range(2):
        value = mxu(sloc[p], cots[p][...], NT)
        for j in range(n):
            ps[j, rank * p : rank * (p + 1), :] = value[:, j * token_piece : (j + 1) * token_piece]
    sent = scatter(ps, pr, ps_s, ps_r)
    pending += sent

    own = []
    for p in range(2):
        for i, target in enumerate((at_x, at_y, at_c)):
            own.append(remote(
                cots[p], gathered[p].at[me], own_send.at[3 * p + i], own_recv.at[3 * p + i], (z, target)
            ))
    start(own)
    pending += own

    loads[0].wait()
    loads[1].wait()
    prior = [mxu(st[p], errs[p][...], NT) for p in range(2)]

    arrived(sent)
    pf[me] = total(ps[me], pr, n - 1)
    sent = spread(pf, pg_s, pg_r)
    pending += sent
    loads[2].wait()
    loads[3].wait()
    arrived(sent)
    for p in range(2):
        value = jnp.concatenate([pf[j, rank * p : rank * (p + 1), :] for j in range(n)], axis=1)
        ls[rank * p : rank * (p + 1), :] = split_dot(value, acts[p][...], NN) + prior[p]
    sent = dp_scatter(ls, lr, ls_s, ls_r)
    pending += sent
    at0[...] = a0[...].T
    arrived(sent)
    lf[mine, :] = total(ls[mine, :], lr, reps - 1) * (1.0 / reps)
    sent = dp_spread(lf, lg_s, lg_r)
    pending += sent
    at1[...] = a1[...].T
    arrived(sent)

    lefts = [lf[rank * p : rank * (p + 1), :] for p in range(2)]
    for p in range(2):
        value = split_dot(lefts[p], acts[p][...], NT)
        for j in range(n):
            qs[j, rank * p : rank * (p + 1), :] = value[:, j * token_piece : (j + 1) * token_piece]
    q_sent = scatter(qs, qr, qs_s, qs_r)
    gs[...] = jnp.zeros_like(gs)
    for p in range(2):
        gs[p, :, 0:rank] = lax.dot_general(
            lefts[p], lefts[p], NT, precision=HIGH, preferred_element_type=jnp.float32
        )
    g_sent = start([
        remote(gs, gr.at[k - 1], gs_s.at[k - 1], gs_r.at[k - 1], shard_peer(k)) for k in range(1, n)
    ])
    cols = ts.shape[2]
    for p in range(2):
        value = split_dot(lefts[p], errs[p][...], NN).astype(jnp.bfloat16)
        for j in range(n):
            ts[j, rank * p : rank * (p + 1), :] = value[:, j * cols : (j + 1) * cols]
    t_sent = scatter(ts, tr, ts_s, ts_r)
    pending += q_sent + g_sent + t_sent

    arrived(q_sent)
    qf[me] = total(qs[me], qr, n - 1)
    sent = spread(qf, qg_s, qg_r)
    pending += sent

    forwards, to_core = [], []
    for p in range(2):
        own[3 * p].wait_recv()
        own[3 * p + 1].wait_recv()
        top, low = pl.ds(0, half), pl.ds(half, half)
        via_y = gathered[p].at[at_x, top]
        via_x = gathered[p].at[at_y, low]
        pair = start([
            remote(via_y, via_y, fwd_send.at[2 * p], fwd_recv.at[2 * p], (z, at_y)),
            remote(via_x, via_x, fwd_send.at[2 * p + 1], fwd_recv.at[2 * p + 1], (z, at_x)),
        ])
        forwards += pair
        to_core += start([
            remote(gathered[p].at[at_x], gathered[p].at[at_x], core_send.at[4 * p], core_recv.at[4 * p], (z, at_c)),
            remote(gathered[p].at[at_y], gathered[p].at[at_y], core_send.at[4 * p + 1], core_recv.at[4 * p + 1], (z, at_c)),
        ])

    arrived(sent)
    arrived(t_sent)
    for p in range(2):
        part = pl.ds(rank * p, rank)
        value = jnp.concatenate([qf[j, rank * p : rank * (p + 1), :] for j in range(n)], axis=1)
        value = split_dot(value, cots[p][...], NN) + ts[me, part, :].astype(jnp.float32)
        for k in range(n - 1):
            value = value + tr[k, part, :].astype(jnp.float32)
        rs[part, :] = value
    sent = dp_scatter(rs, rr, rs_s, rs_r)
    pending += sent
    arrived(g_sent)
    arrived(sent)
    rd[mine, :] = total(rs[mine, :], rr, reps - 1) * (1.0 / reps)
    sent = dp_spread(rd, rg_s, rg_r)
    pending += sent
    arrived(sent)
    rf[me] = rd[...].astype(jnp.bfloat16)
    sent = spread(rf, rf_s, rf_r)
    pending += sent
    grams = [total(gs[p, :, 0:rank], [gr[k, p, :, 0:rank] for k in range(n - 1)], n - 1) for p in range(2)]
    for p in range(2):
        lg[rank * p : rank * (p + 1), :] = lax.dot_general(
            spd_inverse(grams[p]), lefts[p], NN, precision=HIGH, preferred_element_type=jnp.float32
        )
    for p in range(2):
        forwards[2 * p].wait_recv()
        forwards[2 * p + 1].wait_recv()
        top, low = pl.ds(0, half), pl.ds(half, half)
        to_core += start([
            remote(gathered[p].at[at_d, part], gathered[p].at[at_d, part],
                   core_send.at[4 * p + 2 + i], core_recv.at[4 * p + 2 + i], (z, at_c))
            for i, part in enumerate((top, low))
        ])
    arrived(sent)
    arrived(to_core)
    own[2].wait_recv()
    own[5].wait_recv()
    for copy in pending + forwards + to_core:
        copy.wait_send()
    loads[4].wait()
    loads[5].wait()


def final_kernel(p, at, b, e, lg, rf, w, e_new, w_new):
    rank = lg.shape[0] // 2
    step = pl.program_id(0)
    part = slice(rank * p, rank * (p + 1))
    columns = jnp.concatenate([b[0], b[1]], axis=1)
    right = jnp.concatenate([rf[0, part, :], rf[1, part, :]], axis=1)
    approx = mxu(two_terms(lg[part, :]), jnp.concatenate([right, right], axis=0), TN)
    full = mxu(at[...], columns, NN) + e[0].astype(jnp.float32)
    e_new[0] = (full - approx).astype(jnp.bfloat16)

    @pl.when(step == lax.axis_index("dp"))
    def _():
        w_new[...] = w[...] - approx


def fast_body(
    hidden_in, context_in, query_cotan, output_cotan,
    query_error, output_error, query_weight, output_weight, start_factors,
):
    n = lax.axis_size("shard")
    reps = lax.axis_size("dp")
    tok, width = hidden_in.shape
    cols = query_cotan.shape[1]
    dout = start_factors.shape[1]
    rank = start_factors.shape[2]
    f32, bf16 = jnp.float32, jnp.bfloat16
    st = jnp.swapaxes(start_factors, 1, 2)
    sloc = jnp.swapaxes(
        lax.dynamic_slice_in_dim(start_factors, lax.axis_index("shard") * cols, cols, 1), 1, 2
    )
    any_spec = pl.BlockSpec(memory_space=pl.ANY)
    vmem = pl.BlockSpec(memory_space=pltpu.VMEM)
    dma = pltpu.SemaphoreType.DMA
    piece = tok // n
    rows = 2 * rank // reps
    wide = 2 * rank
    g0, g1, at0, at1, lg, rf = pl.pallas_call(
        functools.partial(chain_kernel, n, reps),
        out_shape=(
            jax.ShapeDtypeStruct((n, tok, cols), bf16),
            jax.ShapeDtypeStruct((n, tok, cols), bf16),
            jax.ShapeDtypeStruct((width, tok), bf16),
            jax.ShapeDtypeStruct((width, tok), bf16),
            jax.ShapeDtypeStruct((wide, width), f32),
            jax.ShapeDtypeStruct((n, wide, cols), bf16),
        ),
        in_specs=[any_spec, any_spec, vmem, vmem, any_spec, any_spec, vmem, vmem],
        out_specs=(any_spec, any_spec, vmem, vmem, vmem, vmem),
        scratch_shapes=[
            pltpu.VMEM((tok, width), bf16),
            pltpu.VMEM((tok, width), bf16),
            pltpu.VMEM((width, dout), bf16),
            pltpu.VMEM((width, dout), bf16),
            pltpu.VMEM((n, wide, piece), f32),
            pltpu.VMEM((n - 1, wide, piece), f32),
            pltpu.VMEM((n, wide, piece), f32),
            pltpu.VMEM((wide, width), f32),
            pltpu.VMEM((reps - 1, rows, width), f32),
            pltpu.VMEM((wide, width), f32),
            pltpu.VMEM((n, wide, piece), f32),
            pltpu.VMEM((n - 1, wide, piece), f32),
            pltpu.VMEM((n, wide, piece), f32),
            pltpu.VMEM((n, wide, cols), bf16),
            pltpu.VMEM((n - 1, wide, cols), bf16),
            pltpu.VMEM((2, rank, 128), f32),
            pltpu.VMEM((n - 1, 2, rank, 128), f32),
            pltpu.VMEM((wide, cols), f32),
            pltpu.VMEM((reps - 1, rows, cols), f32),
            pltpu.VMEM((wide, cols), f32),
            dma((6,)), dma((6,)), dma((6,)), dma((4,)), dma((4,)), dma((8,)), dma((8,)),
        ]
        + [dma((n - 1,))] * 4 + [dma((reps - 1,))] * 4
        + [dma((n - 1,))] * 8 + [dma((reps - 1,))] * 4 + [dma((n - 1,))] * 2,
        compiler_params=pltpu.CompilerParams(
            collective_id=0, has_side_effects=True, vmem_limit_bytes=48 * 1024 * 1024
        ),
    )(
        hidden_in, context_in, query_cotan, output_cotan,
        query_error[0], output_error[0], st, sloc,
    )

    span = 2 * cols

    def final(p, at, gathered, error, weight):
        return pl.pallas_call(
            functools.partial(final_kernel, p),
            grid=(dout // span,),
            in_specs=[
                pl.BlockSpec((width, tok), lambda i: (0, 0)),
                pl.BlockSpec((2, tok, cols), lambda i: (i, 0, 0)),
                pl.BlockSpec((1, width, span), lambda i: (0, 0, i)),
                pl.BlockSpec((wide, width), lambda i: (0, 0)),
                pl.BlockSpec((2, wide, cols), lambda i: (i, 0, 0)),
                pl.BlockSpec((width, span), lambda i: (0, 0)),
            ],
            out_specs=(
                pl.BlockSpec((1, width, span), lambda i: (0, 0, i)),
                pl.BlockSpec((width, span), lambda i: (0, 0)),
            ),
            out_shape=(
                jax.ShapeDtypeStruct(error.shape, error.dtype),
                jax.ShapeDtypeStruct(weight.shape, weight.dtype),
            ),
            compiler_params=pltpu.CompilerParams(vmem_limit_bytes=48 * 1024 * 1024),
        )(at, gathered, error, lg, rf, weight)

    query_error_new, query_weight_new = final(0, at0, g0, query_error, query_weight)
    output_error_new, output_weight_new = final(1, at1, g1, output_error, output_weight)
    return (query_error_new, output_error_new, query_weight_new, output_weight_new)


def solution(mesh):
    placed = (
        P("dp", "shard"),
        P("dp", "shard"),
        P("dp", "shard"),
        P("dp", "shard"),
        P("dp", "shard", None),
        P("dp", "shard", None),
        P("shard", "dp"),
        P("shard", "dp"),
        P(),
    )
    return jax.shard_map(
        fast_body if mesh.shape["shard"] == 8 and mesh.shape["dp"] == 4 else body,
        mesh=mesh,
        in_specs=placed,
        out_specs=(
            P("dp", "shard", None),
            P("dp", "shard", None),
            P("shard", "dp"),
            P("shard", "dp"),
        ),
        check_vma=False,
    )
```

profile of v0, /device:TPU:0, one launch (start us, length us, event | category | flops | bytes accessed | tf_op | source)
XLA Modules:
  0.0 117.5 jit_solution(17509697549102311752)
XLA Ops:
  0.6 0.0 copy-start.2
  0.6 0.0 copy-start.3
  0.7 1.0 dynamic-slice_bitcast_fusion.sloc
  1.7 1.4 %copy.13.b0 = bf16[1024,320]{1,0:T(8,128)(2,1)S(1)} copy(bf16[1024,320]{0,1:T(8,128)(2,1)} %param.11) | data formatting | bytes 1310720 | tf_op args[2]
  3.1 0.0 copy-done.3
  3.1 0.4 copy.14.b1
  3.5 0.0 copy-done.2
  3.5 0.0 copy-start
  3.5 94.5 %shard_map.120 = (bf16[8,1024,320]{2,1,0:T(8,128)(2,1)}, bf16[8,1024,320]{2,1,0:T(8,128)(2,1)}, bf16[640,1024]{1,0:T(8,128)(2,1)S(1)}, bf16[640,1024]{1,0:T(8,12...) custom-call(bf16[1024,640]{1,0:T(8,128)(2,1)} %a0_hbm.1, bf16[1024,640]{1,0:T(8,128)(2,1)} %a1_hbm.1, ...), custom_call_target="tpu_custom_call" | custom-call | tf_op jit(solution)/shard_map/pallas_call | solution.py:406
  98.0 0.0 copy-done
  98.1 0.0 copy-start.1
  98.1 9.8 %shard_map.121 = (bf16[1,640,2560]{2,1,0:T(8,128)(2,1)}, f32[640,640]{1,0:T(8,128)}) custom-call(bf16[640,1024]{1,0:T(8,128)(2,1)S(1)} %get-tuple-element.14.at, bf16[8,1024,320]{2,1,0:T(8,128)(2,1)} %get-tuple-element.15.b, bf16[1,640,2560]{2,1,0:T(8,128)(2,1)} %e.2, f32[64,640]{1,0:T(8,128)S(1)} %get-tuple-element.16.lg, ...), custom_call_target="tpu_custom_call" | custom-call | tf_op jit(solution)/shard_map/pallas_call | solution.py:454
  107.8 0.0 copy-done.1
  107.9 9.7 %shard_map.122 = (bf16[1,640,2560]{2,1,0:T(8,128)(2,1)}, f32[640,640]{1,0:T(8,128)}) custom-call(bf16[640,1024]{1,0:T(8,128)(2,1)S(1)} %get-tuple-element.19.at, bf16[8,1024,320]{2,1,0:T(8,128)(2,1)} %get-tuple-element.20.b, bf16[1,640,2560]{2,1,0:T(8,128)(2,1)} %e.3, f32[64,640]{1,0:T(8,128)S(1)} %get-tuple-element.16.lg, ...), custom_call_target="tpu_custom_call" | custom-call | tf_op jit(solution)/shard_map/pallas_call | solution.py:454
Async XLA Ops:
  0.6 2.9 %copy-start.2 = (bf16[2,2560,32]{1,2,0:T(8,128)(2,1)S(1)}, bf16[2,2560,32]{1,2,0:T(8,128)(2,1)}, u32[]{:S(2)}) copy-start(bf16[2,2560,32]{1,2,0:T(8,128)(2,1)} %param.17) | copy-start | bytes 983044
  0.6 2.5 %copy-start.3 = (bf16[1024,320]{0,1:T(8,128)(2,1)S(1)}, bf16[1024,320]{0,1:T(8,128)(2,1)}, u32[]{:S(2)}) copy-start(bf16[1024,320]{0,1:T(8,128)(2,1)} %param.12) | copy-start | bytes 1966084
  3.5 94.5 %copy-start = (f32[640,640]{1,0:T(8,128)S(1)}, f32[640,640]{1,0:T(8,128)}, u32[]{:S(2)}) copy-start(f32[640,640]{1,0:T(8,128)} %w.2) | copy-start | bytes 4915204
  98.1 9.8 %copy-start.1 = (f32[640,640]{1,0:T(8,128)S(1)}, f32[640,640]{1,0:T(8,128)}, u32[]{:S(2)}) copy-start(f32[640,640]{1,0:T(8,128)} %w.3) | copy-start | bytes 4915204
where the time goes:
time: 118 us
  Pallas kernels  114 us (97%)
  local copies, waits for them, and re-layouts  2.83 us (2%)
    pallas_call x1, Pallas kernels, fast_body(): pl.pallas_call(functools.partial(chain_kernel, n, reps), out_shape=(jax.S...  94.5 us
    pallas_call x2, Pallas kernels, final(): pl.pallas_call(functools.partial(final_kernel, p), grid=(dout // span,),...  19.4 us

commit v1 on v0

--- a/solution.py
+++ b/solution.py
@@ -143,8 +143,8 @@
 def chain_kernel(
     n, reps,
     a0_hbm, a1_hbm, b0, b1, e0_hbm, e1_hbm, st, sloc,
-    g0, g1, at0, at1, lg, rf,
-    a0, a1, e0, e1, ps, pr, pf, ls, lr, lf, qs, qr, qf, ts, tr, gs, gr, rs, rr, rd,
+    g0, g1, at0, at1, lg, right,
+    bt0, bt1, rf, a0, a1, e0, e1, ps, pr, pf, ls, lr, lf, qs, qr, qf, ts, tr, gs, gr, rs, rr, rd,
     load_sem, own_send, own_recv, fwd_send, fwd_recv, core_send, core_recv,
     ps_s, ps_r, pg_s, pg_r, ls_s, ls_r, lg_s, lg_r,
     qs_s, qs_r, qg_s, qg_r, ts_s, ts_r, gs_s, gs_r,
@@ -153,14 +153,13 @@
     me = lax.axis_index("shard")
     z = lax.axis_index("dp")
     rank = st.shape[1]
-    rows = 2 * rank // reps
-    acts, errs, cots, gathered = (a0, a1), (e0, e1), (b0, b1), (g0, g1)
-    half = b0.shape[0] // 2
+    acts, errs, cots, gathered = (a0, a1), (e0, e1), (bt0, bt1), (g0, g1)
+    half = b0.shape[1] // 2
 
     loads = [
         pltpu.make_async_copy(src, dst, load_sem.at[i])
         for i, (src, dst) in enumerate(
-            ((e0_hbm, e0), (e1_hbm, e1), (a0_hbm, a0), (a1_hbm, a1), (b0, g0.at[me]), (b1, g1.at[me]))
+            ((e0_hbm, e0), (e1_hbm, e1), (a0_hbm, a0), (a1_hbm, a1))
         )
     ]
     for load in loads:
@@ -171,6 +170,11 @@
         pl.semaphore_signal(barrier, inc=1, device_id=(z, lax.rem(me + k, n)), device_id_type=MESH)
     for k in range(1, reps):
         pl.semaphore_signal(barrier, inc=1, device_id=(lax.rem(z + k, reps), me), device_id_type=MESH)
+    bt0[...] = b0[...].T
+    bt1[...] = b1[...].T
+    kept = [pltpu.make_async_copy(cots[p], gathered[p].at[me], load_sem.at[4 + p]) for p in range(2)]
+    for copy in kept:
+        copy.start()
     pl.semaphore_wait(barrier, n - 1 + reps - 1)
 
     def remote(src, dst, ss, rsem, target):
@@ -212,7 +216,12 @@
             value = value + parts[k].astype(jnp.float32)
         return value
 
+    def own_rows(buf):
+        rows = buf.shape[0] // reps
+        return pl.ds(pl.multiple_of(z * rows, rows), rows)
+
     def dp_scatter(src, dst, ss, rsem):
+        rows = src.shape[0] // reps
         return start([
             remote(
                 src.at[pl.ds(pl.multiple_of(lax.rem(z + k, reps) * rows, rows), rows)],
@@ -221,9 +230,8 @@
             for k in range(1, reps)
         ])
 
-    mine = pl.ds(pl.multiple_of(z * rows, rows), rows)
-
     def dp_spread(buf, ss, rsem):
+        mine = own_rows(buf)
         return start([
             remote(buf.at[mine], buf.at[mine], ss.at[k - 1], rsem.at[k - 1], dp_peer(k))
             for k in range(1, reps)
@@ -240,7 +248,7 @@
 
     token_piece = ps.shape[2]
     for p in range(2):
-        value = mxu(sloc[p], cots[p][...], NT)
+        value = mxu(sloc[p], cots[p][...], NN).astype(jnp.bfloat16)
         for j in range(n):
             ps[j, rank * p : rank * (p + 1), :] = value[:, j * token_piece : (j + 1) * token_piece]
     sent = scatter(ps, pr, ps_s, ps_r)
@@ -252,15 +260,32 @@
             own.append(remote(
                 cots[p], gathered[p].at[me], own_send.at[3 * p + i], own_recv.at[3 * p + i], (z, target)
             ))
-    start(own)
+    start(own[:3])
     pending += own
+
+    forwards, to_core = [], []
+
+    def forward(p):
+        own[3 * p].wait_recv()
+        own[3 * p + 1].wait_recv()
+        top, low = pl.ds(0, half), pl.ds(half, half)
+        via_y = gathered[p].at[at_x, top]
+        via_x = gathered[p].at[at_y, low]
+        forwards.extend(start([
+            remote(via_y, via_y, fwd_send.at[2 * p], fwd_recv.at[2 * p], (z, at_y)),
+            remote(via_x, via_x, fwd_send.at[2 * p + 1], fwd_recv.at[2 * p + 1], (z, at_x)),
+        ]))
+        to_core.extend(start([
+            remote(gathered[p].at[at_x], gathered[p].at[at_x], core_send.at[4 * p], core_recv.at[4 * p], (z, at_c)),
+            remote(gathered[p].at[at_y], gathered[p].at[at_y], core_send.at[4 * p + 1], core_recv.at[4 * p + 1], (z, at_c)),
+        ]))
 
     loads[0].wait()
     loads[1].wait()
     prior = [mxu(st[p], errs[p][...], NT) for p in range(2)]
 
     arrived(sent)
-    pf[me] = total(ps[me], pr, n - 1)
+    pf[me] = total(ps[me].astype(jnp.float32), pr, n - 1).astype(jnp.bfloat16)
     sent = spread(pf, pg_s, pg_r)
     pending += sent
     loads[2].wait()
@@ -268,86 +293,73 @@
     arrived(sent)
     for p in range(2):
         value = jnp.concatenate([pf[j, rank * p : rank * (p + 1), :] for j in range(n)], axis=1)
-        ls[rank * p : rank * (p + 1), :] = split_dot(value, acts[p][...], NN) + prior[p]
+        ls[rank * p : rank * (p + 1), :] = mxu(value, acts[p][...], NN) + prior[p]
     sent = dp_scatter(ls, lr, ls_s, ls_r)
+    start(own[3:])
     pending += sent
     at0[...] = a0[...].T
     arrived(sent)
+    mine = own_rows(ls)
     lf[mine, :] = total(ls[mine, :], lr, reps - 1) * (1.0 / reps)
     sent = dp_spread(lf, lg_s, lg_r)
     pending += sent
     at1[...] = a1[...].T
+    forward(0)
     arrived(sent)
 
     lefts = [lf[rank * p : rank * (p + 1), :] for p in range(2)]
     for p in range(2):
-        value = split_dot(lefts[p], acts[p][...], NT)
+        value = split_dot(lefts[p], acts[p][...], NT).astype(jnp.bfloat16)
         for j in range(n):
             qs[j, rank * p : rank * (p + 1), :] = value[:, j * token_piece : (j + 1) * token_piece]
     q_sent = scatter(qs, qr, qs_s, qs_r)
     gs[...] = jnp.zeros_like(gs)
     for p in range(2):
-        gs[p, :, 0:rank] = lax.dot_general(
+        gs[:, rank * p : rank * (p + 1)] = lax.dot_general(
             lefts[p], lefts[p], NT, precision=HIGH, preferred_element_type=jnp.float32
         )
     g_sent = start([
         remote(gs, gr.at[k - 1], gs_s.at[k - 1], gs_r.at[k - 1], shard_peer(k)) for k in range(1, n)
     ])
-    cols = ts.shape[2]
+    cols = bt0.shape[0]
     for p in range(2):
         value = split_dot(lefts[p], errs[p][...], NN).astype(jnp.bfloat16)
         for j in range(n):
-            ts[j, rank * p : rank * (p + 1), :] = value[:, j * cols : (j + 1) * cols]
+            ts[j, :, cols * p : cols * (p + 1)] = value[:, j * cols : (j + 1) * cols]
     t_sent = scatter(ts, tr, ts_s, ts_r)
     pending += q_sent + g_sent + t_sent
 
     arrived(q_sent)
-    qf[me] = total(qs[me], qr, n - 1)
+    qf[me] = total(qs[me].astype(jnp.float32), qr, n - 1).astype(jnp.bfloat16)
     sent = spread(qf, qg_s, qg_r)
     pending += sent
 
-    forwards, to_core = [], []
-    for p in range(2):
-        own[3 * p].wait_recv()
-        own[3 * p + 1].wait_recv()
-        top, low = pl.ds(0, half), pl.ds(half, half)
-        via_y = gathered[p].at[at_x, top]
-        via_x = gathered[p].at[at_y, low]
-        pair = start([
-            remote(via_y, via_y, fwd_send.at[2 * p], fwd_recv.at[2 * p], (z, at_y)),
-            remote(via_x, via_x, fwd_send.at[2 * p + 1], fwd_recv.at[2 * p + 1], (z, at_x)),
-        ])
-        forwards += pair
-        to_core += start([
-            remote(gathered[p].at[at_x], gathered[p].at[at_x], core_send.at[4 * p], core_recv.at[4 * p], (z, at_c)),
-            remote(gathered[p].at[at_y], gathered[p].at[at_y], core_send.at[4 * p + 1], core_recv.at[4 * p + 1], (z, at_c)),
-        ])
+    forward(1)
 
     arrived(sent)
     arrived(t_sent)
     for p in range(2):
-        part = pl.ds(rank * p, rank)
         value = jnp.concatenate([qf[j, rank * p : rank * (p + 1), :] for j in range(n)], axis=1)
-        value = split_dot(value, cots[p][...], NN) + ts[me, part, :].astype(jnp.float32)
-        for k in range(n - 1):
-            value = value + tr[k, part, :].astype(jnp.float32)
-        rs[part, :] = value
+        rs[:, cols * p : cols * (p + 1)] = mxu(value, cots[p][...], NT)
+    rs[...] = total(rs[...] + ts[me].astype(jnp.float32), tr, n - 1)
     sent = dp_scatter(rs, rr, rs_s, rs_r)
     pending += sent
     arrived(g_sent)
-    arrived(sent)
-    rd[mine, :] = total(rs[mine, :], rr, reps - 1) * (1.0 / reps)
-    sent = dp_spread(rd, rg_s, rg_r)
-    pending += sent
-    arrived(sent)
-    rf[me] = rd[...].astype(jnp.bfloat16)
-    sent = spread(rf, rf_s, rf_r)
-    pending += sent
-    grams = [total(gs[p, :, 0:rank], [gr[k, p, :, 0:rank] for k in range(n - 1)], n - 1) for p in range(2)]
+    gram = total(gs[...], gr, n - 1)
+    grams = [gram[:, rank * p : rank * (p + 1)] for p in range(2)]
     for p in range(2):
         lg[rank * p : rank * (p + 1), :] = lax.dot_general(
             spd_inverse(grams[p]), lefts[p], NN, precision=HIGH, preferred_element_type=jnp.float32
         )
+    arrived(sent)
+    mine = own_rows(rs)
+    rd[mine, :] = total(rs[mine, :], rr, reps - 1) * (1.0 / reps)
+    sent = dp_spread(rd, rg_s, rg_r)
+    pending += sent
+    arrived(sent)
+    rf[me] = rd[...].astype(jnp.bfloat16)
+    sent = spread(rf, rf_s, rf_r)
+    pending += sent
     for p in range(2):
         forwards[2 * p].wait_recv()
         forwards[2 * p + 1].wait_recv()
@@ -358,28 +370,43 @@
             for i, part in enumerate((top, low))
         ])
     arrived(sent)
+    for j in range(n):
+        for p in range(2):
+            right[rank * p : rank * (p + 1), cols * j : cols * (j + 1)] = rf[j, :, cols * p : cols * (p + 1)]
     arrived(to_core)
     own[2].wait_recv()
     own[5].wait_recv()
     for copy in pending + forwards + to_core:
         copy.wait_send()
-    loads[4].wait()
-    loads[5].wait()
-
-
-def final_kernel(p, at, b, e, lg, rf, w, e_new, w_new):
+    for copy in kept:
+        copy.wait()
+
+
+def final_kernel(steps, at0, at1, b0, b1, e0, e1, w0, w1, lg, right, e0_new, e1_new, w0_new, w1_new):
     rank = lg.shape[0] // 2
     step = pl.program_id(0)
-    part = slice(rank * p, rank * (p + 1))
-    columns = jnp.concatenate([b[0], b[1]], axis=1)
-    right = jnp.concatenate([rf[0, part, :], rf[1, part, :]], axis=1)
-    approx = mxu(two_terms(lg[part, :]), jnp.concatenate([right, right], axis=0), TN)
-    full = mxu(at[...], columns, NN) + e[0].astype(jnp.float32)
-    e_new[0] = (full - approx).astype(jnp.bfloat16)
-
-    @pl.when(step == lax.axis_index("dp"))
+    z = lax.axis_index("dp")
+
+    def part(p, place, at, b, e, w, e_new, w_new):
+        span, narrow = b.shape[0], w.shape[1]
+        rows = slice(rank * p, rank * (p + 1))
+        left = two_terms(lg[rows, :])
+
+        def approx(start, size):
+            block = right[rows, pl.ds(pl.multiple_of(start, 128), size)]
+            return mxu(left, jnp.concatenate([block, block], axis=0), TN)
+
+        full = mxu(at[...], b[...], NT) + e[0].astype(jnp.float32)
+        e_new[0] = (full - approx(place * span, span)).astype(jnp.bfloat16)
+        w_new[...] = w[...] - approx((z * steps + place) * narrow, narrow)
+
+    @pl.when(step < steps)
     def _():
-        w_new[...] = w[...] - approx
+        part(0, step, at0, b0, e0, w0, e0_new, w0_new)
+
+    @pl.when(step >= steps)
+    def _():
+        part(1, step - steps, at1, b1, e1, w1, e1_new, w1_new)
 
 
 def fast_body(
@@ -401,41 +428,45 @@
     vmem = pl.BlockSpec(memory_space=pltpu.VMEM)
     dma = pltpu.SemaphoreType.DMA
     piece = tok // n
-    rows = 2 * rank // reps
     wide = 2 * rank
-    g0, g1, at0, at1, lg, rf = pl.pallas_call(
+    rows = wide // reps
+    pair = 2 * cols
+    g0, g1, at0, at1, lg, right = pl.pallas_call(
         functools.partial(chain_kernel, n, reps),
         out_shape=(
-            jax.ShapeDtypeStruct((n, tok, cols), bf16),
-            jax.ShapeDtypeStruct((n, tok, cols), bf16),
+            jax.ShapeDtypeStruct((n, cols, tok), bf16),
+            jax.ShapeDtypeStruct((n, cols, tok), bf16),
             jax.ShapeDtypeStruct((width, tok), bf16),
             jax.ShapeDtypeStruct((width, tok), bf16),
             jax.ShapeDtypeStruct((wide, width), f32),
-            jax.ShapeDtypeStruct((n, wide, cols), bf16),
+            jax.ShapeDtypeStruct((wide, dout), bf16),
         ),
         in_specs=[any_spec, any_spec, vmem, vmem, any_spec, any_spec, vmem, vmem],
         out_specs=(any_spec, any_spec, vmem, vmem, vmem, vmem),
         scratch_shapes=[
+            pltpu.VMEM((cols, tok), bf16),
+            pltpu.VMEM((cols, tok), bf16),
+            pltpu.VMEM((n, rank, pair), bf16),
             pltpu.VMEM((tok, width), bf16),
             pltpu.VMEM((tok, width), bf16),
             pltpu.VMEM((width, dout), bf16),
             pltpu.VMEM((width, dout), bf16),
-            pltpu.VMEM((n, wide, piece), f32),
-            pltpu.VMEM((n - 1, wide, piece), f32),
-            pltpu.VMEM((n, wide, piece), f32),
+            pltpu.VMEM((n, wide, piece), bf16),
+            pltpu.VMEM((n - 1, wide, piece), bf16),
+            pltpu.VMEM((n, wide, piece), bf16),
             pltpu.VMEM((wide, width), f32),
             pltpu.VMEM((reps - 1, rows, width), f32),
             pltpu.VMEM((wide, width), f32),
-            pltpu.VMEM((n, wide, piece), f32),
-            pltpu.VMEM((n - 1, wide, piece), f32),
-            pltpu.VMEM((n, wide, piece), f32),
-            pltpu.VMEM((n, wide, cols), bf16),
-            pltpu.VMEM((n - 1, wide, cols), bf16),
-            pltpu.VMEM((2, rank, 128), f32),
-            pltpu.VMEM((n - 1, 2, rank, 128), f32),
-            pltpu.VMEM((wide, cols), f32),
-            pltpu.VMEM((reps - 1, rows, cols), f32),
-            pltpu.VMEM((wide, cols), f32),
+            pltpu.VMEM((n, wide, piece), bf16),
+            pltpu.VMEM((n - 1, wide, piece), bf16),
+            pltpu.VMEM((n, wide, piece), bf16),
+            pltpu.VMEM((n, rank, pair), bf16),
+            pltpu.VMEM((n - 1, rank, pair), bf16),
+            pltpu.VMEM((rank, 128), f32),
+            pltpu.VMEM((n - 1, rank, 128), f32),
+            pltpu.VMEM((rank, pair), f32),
+            pltpu.VMEM((reps - 1, rank // reps, pair), f32),
+            pltpu.VMEM((rank, pair), f32),
             dma((6,)), dma((6,)), dma((6,)), dma((4,)), dma((4,)), dma((8,)), dma((8,)),
         ]
         + [dma((n - 1,))] * 4 + [dma((reps - 1,))] * 4
@@ -448,34 +479,36 @@
         query_error[0], output_error[0], st, sloc,
     )
 
-    span = 2 * cols
-
-    def final(p, at, gathered, error, weight):
-        return pl.pallas_call(
-            functools.partial(final_kernel, p),
-            grid=(dout // span,),
-            in_specs=[
-                pl.BlockSpec((width, tok), lambda i: (0, 0)),
-                pl.BlockSpec((2, tok, cols), lambda i: (i, 0, 0)),
-                pl.BlockSpec((1, width, span), lambda i: (0, 0, i)),
-                pl.BlockSpec((wide, width), lambda i: (0, 0)),
-                pl.BlockSpec((2, wide, cols), lambda i: (i, 0, 0)),
-                pl.BlockSpec((width, span), lambda i: (0, 0)),
-            ],
-            out_specs=(
-                pl.BlockSpec((1, width, span), lambda i: (0, 0, i)),
-                pl.BlockSpec((width, span), lambda i: (0, 0)),
-            ),
-            out_shape=(
-                jax.ShapeDtypeStruct(error.shape, error.dtype),
-                jax.ShapeDtypeStruct(weight.shape, weight.dtype),
-            ),
-            compiler_params=pltpu.CompilerParams(vmem_limit_bytes=48 * 1024 * 1024),
-        )(at, gathered, error, lg, rf, weight)
-
-    query_error_new, query_weight_new = final(0, at0, g0, query_error, query_weight)
-    output_error_new, output_weight_new = final(1, at1, g1, output_error, output_weight)
-    return (query_error_new, output_error_new, query_weight_new, output_weight_new)
+    span = dout // 5
+
+    steps = dout // span
+    narrow = query_weight.shape[1] // steps
+
+    def first(i):
+        return jnp.minimum(i, steps - 1)
+
+    def second(i):
+        return jnp.maximum(i - steps, 0)
+
+    def whole(shape):
+        return pl.BlockSpec(shape, lambda i: (0, 0))
+
+    err_specs = [pl.BlockSpec((1, width, span), lambda i, at=at: (0, 0, at(i))) for at in (first, second)]
+    w_specs = [pl.BlockSpec((width, narrow), lambda i, at=at: (0, at(i))) for at in (first, second)]
+    b_specs = [pl.BlockSpec((span, tok), lambda i, at=at: (at(i), 0)) for at in (first, second)]
+    outs = (query_error, output_error, query_weight, output_weight)
+    return pl.pallas_call(
+        functools.partial(final_kernel, steps),
+        grid=(2 * steps,),
+        in_specs=[whole((width, tok))] * 2 + b_specs + err_specs + w_specs
+        + [whole((wide, width)), whole((wide, dout))],
+        out_specs=tuple(err_specs + w_specs),
+        out_shape=tuple(jax.ShapeDtypeStruct(out.shape, out.dtype) for out in outs),
+        compiler_params=pltpu.CompilerParams(vmem_limit_bytes=48 * 1024 * 1024),
+    )(
+        at0, at1, g0.reshape(dout, tok), g1.reshape(dout, tok),
+        query_error, output_error, query_weight, output_weight, lg, right,
+    )
 
 
 def solution(mesh):

time: 118 us -> 96.9 us (0.82)
  Pallas kernels: 114 us -> 92.9 us
    pallas_call x1, Pallas kernels: 94.5 us -> 75.5 us  [fast_body(): pl.pallas_call(functools.partial(chain_kernel, n, reps), out_shape=(jax.S...]
    pallas_call x2 -> x1, Pallas kernels: 19.4 us -> 17.5 us  [fast_body(): pl.pallas_call(functools.partial(final_kernel, steps), grid=(2 * steps,),...]
where the time goes in v1:
time: 96.9 us; the launch traced here: 96.5 us
  Pallas kernels  92.9 us (96%)
  local copies, waits for them, and re-layouts  2.82 us (3%)
    pallas_call x1, Pallas kernels, fast_body(): pl.pallas_call(functools.partial(chain_kernel, n, reps), out_shape=(jax.S...  75.5 us
    pallas_call x1, Pallas kernels, fast_body(): pl.pallas_call(functools.partial(final_kernel, steps), grid=(2 * steps,),...  17.5 us

profile of v1, /device:TPU:0, one launch (start us, length us, event | category | flops | bytes accessed | tf_op | source)
XLA Modules:
  0.0 96.5 jit_solution(17223007241936445026)
XLA Ops:
  0.6 0.0 copy-start.1
  0.6 0.0 copy-start.2
  0.7 1.0 %dynamic-slice_bitcast_fusion.sloc = bf16[2,32,320]{2,1,0:T(8,128)(2,1)S(1)} fusion(bf16[2,2560,32]{1,2,0:T(8,128)(2,1)} %param.17, s32[]{:T(128)S(6)} %select_n.3), kind=kLoop, calls=%fused_computation | loop fusion | bytes 81924 | tf_op jit(solution)/shard_map/transpose | solution.py:424
  1.7 1.4 %copy.13.b0 = bf16[1024,320]{1,0:T(8,128)(2,1)S(1)} copy(bf16[1024,320]{0,1:T(8,128)(2,1)} %param.11) | data formatting | bytes 1310720 | tf_op args[2]
  3.1 0.0 copy-done.2
  3.1 0.4 copy.14.b1
  3.5 0.0 copy-done.1
  3.5 0.0 copy-start
  3.5 75.5 %shard_map.120 = (bf16[8,320,1024]{2,1,0:T(8,128)(2,1)}, bf16[8,320,1024]{2,1,0:T(8,128)(2,1)}, bf16[640,1024]{1,0:T(8,128)(2,1)S(1)}, bf16[640,1024]{1,0:T(8,12...) custom-call(bf16[1024,640]{1,0:T(8,128)(2,1)} %a0_hbm.1, bf16[1024,640]{1,0:T(8,128)(2,1)} %a1_hbm.1, ...), custom_call_target="tpu_custom_call" | custom-call | tf_op jit(solution)/shard_map/pallas_call | solution.py:434
  79.0 0.0 copy-done
  79.0 17.5 %shard_map.121 = (bf16[1,640,2560]{2,1,0:T(8,128)(2,1)}, bf16[1,640,2560]{2,1,0:T(8,128)(2,1)}, f32[640,640]{1,0:T(8,128)}, f32[640,640]{1,0:T(8,128)}) custom-call(bf16[640,1024]{1,0:T(8,128)(2,1)S(1)} %get-tuple-element.10.at0, bf16[640,1024]{1,0:T(8,128)(2,1)S(1)} %get-tuple-element.11.at1, bf16[2560,1024]{1,0:T(8,128)(2,1)} %bitcast.10, ...), custom_call_target="tpu_custom_call" | custom-call | tf_op jit(solution)/shard_map/pallas_call | solution.py:500
Async XLA Ops:
  0.6 2.9 %copy-start.1 = (bf16[2,2560,32]{1,2,0:T(8,128)(2,1)S(1)}, bf16[2,2560,32]{1,2,0:T(8,128)(2,1)}, u32[]{:S(2)}) copy-start(bf16[2,2560,32]{1,2,0:T(8,128)(2,1)} %param.17) | copy-start | bytes 983044
  0.6 2.5 %copy-start.2 = (bf16[1024,320]{0,1:T(8,128)(2,1)S(1)}, bf16[1024,320]{0,1:T(8,128)(2,1)}, u32[]{:S(2)}) copy-start(bf16[1024,320]{0,1:T(8,128)(2,1)} %param.12) | copy-start | bytes 1966084
  3.5 75.5 %copy-start = (f32[640,640]{1,0:T(8,128)S(1)}, f32[640,640]{1,0:T(8,128)}, u32[]{:S(2)}) copy-start(f32[640,640]{1,0:T(8,128)} %w0.1) | copy-start | bytes 4915204

commit v2 on v1

--- a/solution.py
+++ b/solution.py
@@ -293,14 +293,14 @@
     arrived(sent)
     for p in range(2):
         value = jnp.concatenate([pf[j, rank * p : rank * (p + 1), :] for j in range(n)], axis=1)
-        ls[rank * p : rank * (p + 1), :] = mxu(value, acts[p][...], NN) + prior[p]
+        ls[rank * p : rank * (p + 1), :] = (mxu(value, acts[p][...], NN) + prior[p]).astype(jnp.bfloat16)
     sent = dp_scatter(ls, lr, ls_s, ls_r)
     start(own[3:])
     pending += sent
     at0[...] = a0[...].T
     arrived(sent)
     mine = own_rows(ls)
-    lf[mine, :] = total(ls[mine, :], lr, reps - 1) * (1.0 / reps)
+    lf[mine, :] = (total(ls[mine, :].astype(jnp.float32), lr, reps - 1) * (1.0 / reps)).astype(jnp.bfloat16)
     sent = dp_spread(lf, lg_s, lg_r)
     pending += sent
     at1[...] = a1[...].T
@@ -309,21 +309,19 @@
 
     lefts = [lf[rank * p : rank * (p + 1), :] for p in range(2)]
     for p in range(2):
-        value = split_dot(lefts[p], acts[p][...], NT).astype(jnp.bfloat16)
+        value = mxu(lefts[p], acts[p][...], NT).astype(jnp.bfloat16)
         for j in range(n):
             qs[j, rank * p : rank * (p + 1), :] = value[:, j * token_piece : (j + 1) * token_piece]
     q_sent = scatter(qs, qr, qs_s, qs_r)
     gs[...] = jnp.zeros_like(gs)
     for p in range(2):
-        gs[:, rank * p : rank * (p + 1)] = lax.dot_general(
-            lefts[p], lefts[p], NT, precision=HIGH, preferred_element_type=jnp.float32
-        )
+        gs[:, rank * p : rank * (p + 1)] = mxu(lefts[p], lefts[p], NT)
     g_sent = start([
         remote(gs, gr.at[k - 1], gs_s.at[k - 1], gs_r.at[k - 1], shard_peer(k)) for k in range(1, n)
     ])
     cols = bt0.shape[0]
     for p in range(2):
-        value = split_dot(lefts[p], errs[p][...], NN).astype(jnp.bfloat16)
+        value = mxu(lefts[p], errs[p][...], NN).astype(jnp.bfloat16)
         for j in range(n):
             ts[j, :, cols * p : cols * (p + 1)] = value[:, j * cols : (j + 1) * cols]
     t_sent = scatter(ts, tr, ts_s, ts_r)
@@ -349,7 +347,7 @@
     grams = [gram[:, rank * p : rank * (p + 1)] for p in range(2)]
     for p in range(2):
         lg[rank * p : rank * (p + 1), :] = lax.dot_general(
-            spd_inverse(grams[p]), lefts[p], NN, precision=HIGH, preferred_element_type=jnp.float32
+            spd_inverse(grams[p]), lefts[p].astype(jnp.float32), NN, precision=HIGH, preferred_element_type=jnp.float32
         )
     arrived(sent)
     mine = own_rows(rs)
@@ -454,9 +452,9 @@
             pltpu.VMEM((n, wide, piece), bf16),
             pltpu.VMEM((n - 1, wide, piece), bf16),
             pltpu.VMEM((n, wide, piece), bf16),
-            pltpu.VMEM((wide, width), f32),
-            pltpu.VMEM((reps - 1, rows, width), f32),
-            pltpu.VMEM((wide, width), f32),
+            pltpu.VMEM((wide, width), bf16),
+            pltpu.VMEM((reps - 1, rows, width), bf16),
+            pltpu.VMEM((wide, width), bf16),
             pltpu.VMEM((n, wide, piece), bf16),
             pltpu.VMEM((n - 1, wide, piece), bf16),
             pltpu.VMEM((n, wide, piece), bf16),

time: 96.9 us -> 96.9 us (level)
  no operation moved by 1% of the time
where the time goes in v2:
time: 96.9 us; the launch traced here: 96.4 us
  Pallas kernels  92.9 us (96%)
  local copies, waits for them, and re-layouts  2.82 us (3%)
    pallas_call x1, Pallas kernels, fast_body(): pl.pallas_call(functools.partial(chain_kernel, n, reps), out_shape=(jax.S...  75.4 us
    pallas_call x1, Pallas kernels, fast_body(): pl.pallas_call(functools.partial(final_kernel, steps), grid=(2 * steps,),...  17.5 us

profile of v2, /device:TPU:0, one launch (start us, length us, event | category | flops | bytes accessed | tf_op | source)
XLA Modules:
  0.0 96.4 jit_solution(10297716744811280580)
XLA Ops:
  0.6 0.0 copy-start.1
  0.6 0.0 copy-start.2
  0.7 1.0 %dynamic-slice_bitcast_fusion.sloc = bf16[2,32,320]{2,1,0:T(8,128)(2,1)S(1)} fusion(bf16[2,2560,32]{1,2,0:T(8,128)(2,1)} %param.17, s32[]{:T(128)S(6)} %select_n.3), kind=kLoop, calls=%fused_computation | loop fusion | bytes 81924 | tf_op jit(solution)/shard_map/transpose | solution.py:422
  1.7 1.4 %copy.13.b0 = bf16[1024,320]{1,0:T(8,128)(2,1)S(1)} copy(bf16[1024,320]{0,1:T(8,128)(2,1)} %param.11) | data formatting | bytes 1310720 | tf_op args[2]
  3.1 0.0 copy-done.2
  3.1 0.4 copy.14.b1
  3.5 0.0 copy-done.1
  3.5 0.0 copy-start
  3.5 75.4 %shard_map.120 = (bf16[8,320,1024]{2,1,0:T(8,128)(2,1)}, bf16[8,320,1024]{2,1,0:T(8,128)(2,1)}, bf16[640,1024]{1,0:T(8,128)(2,1)S(1)}, bf16[640,1024]{1,0:T(8,12...) custom-call(bf16[1024,640]{1,0:T(8,128)(2,1)} %a0_hbm.1, bf16[1024,640]{1,0:T(8,128)(2,1)} %a1_hbm.1, ...), custom_call_target="tpu_custom_call" | custom-call | tf_op jit(solution)/shard_map/pallas_call | solution.py:432
  79.0 0.0 copy-done
  79.0 17.5 %shard_map.121 = (bf16[1,640,2560]{2,1,0:T(8,128)(2,1)}, bf16[1,640,2560]{2,1,0:T(8,128)(2,1)}, f32[640,640]{1,0:T(8,128)}, f32[640,640]{1,0:T(8,128)}) custom-call(bf16[640,1024]{1,0:T(8,128)(2,1)S(1)} %get-tuple-element.10.at0, bf16[640,1024]{1,0:T(8,128)(2,1)S(1)} %get-tuple-element.11.at1, bf16[2560,1024]{1,0:T(8,128)(2,1)} %bitcast.10, ...), custom_call_target="tpu_custom_call" | custom-call | tf_op jit(solution)/shard_map/pallas_call | solution.py:498
Async XLA Ops:
  0.6 2.9 %copy-start.1 = (bf16[2,2560,32]{1,2,0:T(8,128)(2,1)S(1)}, bf16[2,2560,32]{1,2,0:T(8,128)(2,1)}, u32[]{:S(2)}) copy-start(bf16[2,2560,32]{1,2,0:T(8,128)(2,1)} %param.17) | copy-start | bytes 983044
  0.6 2.5 %copy-start.2 = (bf16[1024,320]{0,1:T(8,128)(2,1)S(1)}, bf16[1024,320]{0,1:T(8,128)(2,1)}, u32[]{:S(2)}) copy-start(bf16[1024,320]{0,1:T(8,128)(2,1)} %param.12) | copy-start | bytes 1966084
  3.5 75.5 %copy-start = (f32[640,640]{1,0:T(8,128)S(1)}, f32[640,640]{1,0:T(8,128)}, u32[]{:S(2)}) copy-start(f32[640,640]{1,0:T(8,128)} %w0.1) | copy-start | bytes 4915204
